TPU v7x, 512 devices: a whole 4x8x8 slice. The times are simulated.
512 devices in a mesh: row: 32 (over y, x), help: 16 (over z, core).
Axes of the slice: x: 4, y: 8, z: 8, core: 2. Of those that a mesh axis runs over, the one named last changes fastest.
Arguments:
- factor_inv: bfloat16 [1024, 1024, 1024], P(('row', 'help'))
- b_rows: int32 [1024, 512], P(('row', 'help')), may hold values from 0 to 1023
- b_coef: float32 [1024, 512], P(('row', 'help')), may hold values from -1 to 1
- b_count: int32 [1024], P(('row', 'help')), may hold values from 128 to 512
- refined: int32 [32, 8], P('row'), may hold values from 0 to 31, as said below
- modes: float32 [1024, 6, 1024], P(('row', 'help')), may hold values from -6 to 6
- owner: int32 [1024, 512], P(('row', 'help')), may hold values from 0 to 511
Outputs:
- dual_blocks: bfloat16 [256, 512, 512], P('row', 'help')
- coarse: float32 [6144, 512], P(None, 'row')
Inputs may be any that keep to these rules, and one draw needn't show every extreme that they name: Each row of refined holds 8 numbers l of different devices' ranges, device d's range being 2 * d to 2 * d + 1, so no device holds more than one listed subdomain.
All inputs are finite; a program needn't handle non-finite values.
Results may differ from a plain program's by a relative error of at most 0.0065.
Values may be sent and summed in bfloat16 or wider, within the bound.
A program may use at most 64 MiB of HBM per device.

v0:
```python
import jax
import jax.numpy as jnp
from jax import lax
from jax.sharding import PartitionSpec as P

LAM_DEV = 16


def assemble(matrix, rows_here, scale):
    picked = jnp.take(matrix, rows_here, axis=1).astype(jnp.float32) * scale[None, :]
    panel = picked.astype(jnp.bfloat16)
    gram = lax.dot_general(
        panel, panel, (((0,), (0,)), ((), ())), preferred_element_type=jnp.float32
    )
    return gram.astype(jnp.bfloat16)


def on_device(factor_inv, b_rows, b_coef, b_count, refined, modes, owner):
    parts = lax.axis_size("help")
    groups = lax.axis_size("row")
    slots = factor_inv.shape[0]
    width = b_rows.shape[1]
    column = lax.broadcasted_iota(jnp.int32, b_rows.shape, 1)
    weights = jnp.where(column < b_count[:, None], b_coef, jnp.float32(0.0))
    listed = refined[0]
    source = listed // slots
    blocks = []
    for slot in range(slots):
        block = assemble(factor_inv[slot], b_rows[slot], weights[slot])
        blocks.append(block)
    stacked = jnp.stack(blocks).reshape(slots, parts, width // parts, width)
    received = lax.all_to_all(stacked, "help", split_axis=1, concat_axis=1, tiled=True)
    which = listed % slots
    dual_blocks = received[which, source]
    mode_count = modes.shape[1]
    total_lam = LAM_DEV * groups
    gather_rows = jnp.broadcast_to(b_rows[:, None, :], (slots, mode_count, width))
    values = jnp.take_along_axis(modes, gather_rows, axis=2) * weights[:, None, :]

    def owner_terms(piece, owned):
        return jnp.zeros((mode_count, total_lam), jnp.float32).at[:, owned].add(piece)

    term = jax.vmap(owner_terms)(values, owner).reshape(slots * mode_count, total_lam)
    grouped = lax.all_gather(term, "help", axis=0, tiled=True)
    coarse = lax.all_to_all(grouped, "row", split_axis=1, concat_axis=0, tiled=True)
    return (dual_blocks, coarse)


def solution(mesh):
    in_specs = (
        P(("row", "help"), None, None),
        P(("row", "help"), None),
        P(("row", "help"), None),
        P(("row", "help")),
        P("row", None),
        P(("row", "help"), None, None),
        P(("row", "help"), None),
    )
    out_specs = (P("row", "help", None), P(None, "row"))
    return jax.shard_map(
        on_device, mesh=mesh, in_specs=in_specs, out_specs=out_specs, check_vma=False
    )
```

profile of v0, /device:TPU:1, one launch (start us, length us, event | category | flops | bytes accessed | tf_op | source)
XLA Modules:
  0.0 168.0 jit_solution(12929017602336620794)
XLA Ops:
  0.6 0.0 copy-start
  0.6 0.7 broadcast_add_fusion
  1.3 0.7 broadcast_compare_fusion
  2.0 0.7 fusion.13
  2.7 0.7 and_reduce_fusion
  3.5 0.7 multiply_reduce_fusion
  4.2 0.7 shift-left_or_fusion
  5.0 0.0 copy-done
  5.0 0.0 copy-start.3
  5.0 0.0 copy-start.4
  5.0 0.0 copy-start.2
  5.0 59.6 %gather_fusion.1 = f32[6144]{0:T(1024)S(1)} fusion(f32[2,6,1024]{2,0,1:T(2,128)S(1)} %copy-done, s32[6144]{0:T(1024)S(1)} %reshape.179), kind=kCustom, calls=%fused_computation.3 | custom fusion | bytes 122880 | tf_op jit(solution)/shard_map/jit(take_along_axis)/gather | solution.py:38
  64.6 0.0 copy-done.3
  64.6 0.0 copy-done.4
  64.6 0.1 compare_select_fusion.1
  64.7 0.0 copy-done.2
  64.7 0.2 copy.24
  64.9 6.2 %scatter_custom_fusion = f32[6,1024]{0,1:T(8,128)S(1)} fusion(s32[1024]{0:T(1024)S(1)} %bitcast.66, f32[1024,6]{1,0:T(8,128)S(1)} %copy.24, f32[]{:T(128)} %constant.51.clone.1), kind=kCustom, calls=%fused_computation.20 | custom fusion | flops 6144 | bytes 24580
  71.1 0.2 copy.25
  71.3 27.3 %all-gather = f32[16,12,512]{2,1,0:T(8,128)} all-gather(f32[1,12,512]{2,1,0:T(8,128)S(1)} %reshape.193), channel_id=1, replica_groups=mesh['row'=32,'help'=16] {'help'}, dimensions={0}, use_global_device_ids=true | all-gather | bytes 417792 | tf_op jit(solution)/shard_map/all_gather | solution.py:44
  98.6 2.1 %all_to_all.18 = f32[192,32,16]{2,1,0:T(8,128)S(1)} reshape(f32[16,12,512]{2,1,0:T(8,128)} %all-gather) | data formatting | bytes 786432 | tf_op jit(solution)/shard_map/all_to_all | solution.py:45
  100.7 2.4 %copy.26 = f32[192,32,16]{0,2,1:T(8,128)} copy(f32[192,32,16]{2,1,0:T(8,128)S(1)} %all_to_all.18) | data formatting | bytes 786432 | tf_op jit(solution)/shard_map/all_to_all | solution.py:45
  103.1 9.7 %all-to-all-start.1 = ((f32[192,32,16]{0,2,1:T(8,128)}), f32[192,32,16]{0,2,1:T(8,128)S(1)}, u32[]{:S(2)}, u32[]{:S(2)}) async-start(f32[192,32,16]{0,2,1:T(8,128)} %copy.26), calls=%async_computation.1 | async-start | bytes 1048576 | tf_op jit(solution)/shard_map/all_to_all | solution.py:45
  112.9 4.6 %fusion.22 = (bf16[1,1024,1024]{2,1,0:T(8,128)(2,1)}, bf16[1,1024,1024]{2,1,0:T(8,128)(2,1)}) fusion(bf16[2,1024,1024]{2,1,0:T(8,128)(2,1)} %param.9), kind=kLoop, calls=%fused_computation.58 | loop fusion | bytes 8388608 | tf_op jit(solution)/shard_map/slice | solution.py:29
  117.5 2.9 %copy.29 = bf16[1,1024,1024]{1,2,0:T(8,128)(2,1)S(1)} copy(bf16[1,1024,1024]{2,1,0:T(8,128)(2,1)} %get-tuple-element.4) | data formatting | bytes 4194304
  120.3 3.9 %copy.28 = bf16[1,1024,1024]{1,2,0:T(8,128)(2,1)} copy(bf16[1,1024,1024]{2,1,0:T(8,128)(2,1)} %get-tuple-element.3) | data formatting | bytes 4194304
  124.3 2.8 %gather_fusion.3 = bf16[512,1024]{1,0:T(8,128)(2,1)} fusion(bf16[1024,1024]{0,1:T(8,128)(2,1)S(1)} %bitcast.54, s32[1024]{0:T(1024)S(1)} %pad_clamp_fusion), kind=kCustom, calls=%fused_computation.1.clone | custom fusion | bytes 2099200 | tf_op jit(solution)/shard_map/jit(_take)/gather | solution.py:10
  127.1 0.0 copy-start.1
  127.1 4.7 %gather_fusion.2 = bf16[512,1024]{1,0:T(8,128)(2,1)S(1)} fusion(bf16[1024,1024]{0,1:T(8,128)(2,1)} %bitcast.55, s32[1024]{0:T(1024)S(1)} %pad_clamp_fusion.1), kind=kCustom, calls=%fused_computation.clone | custom fusion | bytes 2099200 | tf_op jit(solution)/shard_map/jit(_take)/gather | solution.py:10
  131.8 0.0 copy-done.1
  131.8 1.0 convolution_convert_fusion
  132.7 0.0 copy-start.5
  132.7 1.0 convolution_convert_fusion.1
  133.7 1.1 pad_maximum_fusion
  134.8 0.0 all-to-all-done.1
  134.8 3.9 %all-to-all-start = ((bf16[2,16,32,512]{3,2,0,1:T(8,128)(2,1)}), bf16[2,16,32,512]{3,2,0,1:T(8,128)(2,1)S(1)}, u32[]{:S(2)}, u32[]{:S(2)}) async-start(bf16[2,16,32,512]{3,2,0,1:T(8,128)(2,1)} %pad_maximum_fusion), calls=%async_computation | async-start | bytes 2097152 | tf_op jit(solution)/shard_map/all_to_all | solution.py:32
  138.6 0.0 copy-done.5
  138.7 0.3 copy.27
  139.0 1.0 all_to_all.21
  139.9 26.7 %all-to-all-done = bf16[2,16,32,512]{3,2,0,1:T(8,128)(2,1)S(1)} async-done(((bf16[2,16,32,512]{3,2,0,1:T(8,128)(2,1)}), bf16[2,16,32,512]{3,2,0,1:T(8,128)(2,1)S(1)}, u32[]{:S(2)}, u32[]{:S(2)}) %all-to-all-start) | async-done | bytes 1048608 | tf_op jit(solution)/shard_map/all_to_all | solution.py:32
  166.6 0.1 copy.23
  166.7 1.3 gather_fusion
  (16 shorter events, 0.1 us)
Async XLA Ops:
  0.6 4.3 %copy-start = (f32[2,6,1024]{2,0,1:T(2,128)S(1)}, f32[2,6,1024]{2,0,1:T(2,128)}, u32[]{:S(2)}) copy-start(f32[2,6,1024]{2,0,1:T(2,128)} %param.14) | copy-start | bytes 147460
  5.0 59.6 %copy-start.3 = (f32[2,512]{1,0:T(2,128)S(1)}, f32[2,512]{1,0:T(2,128)}, u32[]{:S(2)}) copy-start(f32[2,512]{1,0:T(2,128)} %param.11) | copy-start | bytes 12292
  5.0 59.6 %copy-start.4 = (s32[2]{0:T(128)S(1)}, s32[2]{0:T(128)}, u32[]{:S(2)}) copy-start(s32[2]{0:T(128)} %param.12) | copy-start | bytes 28
  5.0 59.7 %copy-start.2 = (s32[2,512]{1,0:T(2,128)S(1)}, s32[2,512]{1,0:T(2,128)}, u32[]{:S(2)}) copy-start(s32[2,512]{1,0:T(2,128)} %param.10) | copy-start | bytes 12292
  103.1 31.7 %all-to-all-start.1 = ((f32[192,32,16]{0,2,1:T(8,128)}), f32[192,32,16]{0,2,1:T(8,128)S(1)}, u32[]{:S(2)}, u32[]{:S(2)}) async-start(f32[192,32,16]{0,2,1:T(8,128)} %copy.26), calls=%async_computation.1 | async-start | bytes 1048576 | tf_op jit(solution)/shard_map/all_to_all | solution.py:45
  127.1 4.7 %copy-start.1 = (bf16[512,1024]{1,0:T(8,128)(2,1)S(1)}, bf16[512,1024]{1,0:T(8,128)(2,1)}, u32[]{:S(2)}) copy-start(bf16[512,1024]{1,0:T(8,128)(2,1)} %gather_fusion.3) | copy-start | bytes 3145732
  132.7 5.9 %copy-start.5 = (s32[1,8]{1,0:T(1,128)S(1)}, s32[1,8]{1,0:T(1,128)}, u32[]{:S(2)}) copy-start(s32[1,8]{1,0:T(1,128)} %param.13) | copy-start | bytes 100
  134.8 31.8 %all-to-all-start = ((bf16[2,16,32,512]{3,2,0,1:T(8,128)(2,1)}), bf16[2,16,32,512]{3,2,0,1:T(8,128)(2,1)S(1)}, u32[]{:S(2)}, u32[]{:S(2)}) async-start(bf16[2,16,32,512]{3,2,0,1:T(8,128)(2,1)} %pad_maximum_fusion), calls=%async_computation | async-start | bytes 2097152 | tf_op jit(solution)/shard_map/all_to_all | solution.py:32
where the time goes:
time: 169 us; the launch traced here: 168 us
  local copies, waits for them, and re-layouts  86 us (51%)
  blocking collectives  27.3 us (16%)
  waiting for transfers between devices  26.7 us (16%)
  starting transfers between devices  13.5 us (8%)
  other arithmetic  11.6 us (7%)
  matrix products  1.92 us (1%)
    gather x3, local copies, waits for them, and re-layouts, on_device(): jnp.take_along_axis(modes, gather_rows, axis=2) * weights[:, None, :]  59.6 us
    all_gather x1, blocking collectives, on_device(): grouped = lax.all_gather(term, 'help', axis=0, tiled=True)  27.3 us
    all_to_all x1, waiting for transfers between devices, on_device(): lax.all_to_all(stacked, 'help', split_axis=1, concat_axis=1, tiled=True)  26.7 us
    all_to_all x1, starting transfers between devices, on_device(): lax.all_to_all(grouped, 'row', split_axis=1, concat_axis=0, tiled=True)  9.67 us
    unnamed x4, other arithmetic  7.64 us
    gather x2, local copies, waits for them, and re-layouts, assemble(): jnp.take(matrix, rows_here, axis=1).astype(jnp.float32) * scale[None, :]  7.45 us
    unnamed x18, local copies, waits for them, and re-layouts  7.03 us
    all_to_all x4, local copies, waits for them, and re-layouts, on_device(): lax.all_to_all(grouped, 'row', split_axis=1, concat_axis=0, tiled=True)  5.75 us
  transfers between devices with their start and end apart: 2, of which 1 were waited for; matrix products, arithmetic and copies ran while one was open for 13% of the time, Pallas kernels for 0%

commit v1 on v0

v1 whole, which is shorter than its diff:
```python
import functools

import jax
import jax.numpy as jnp
from jax import lax
from jax.experimental import pallas as pl
from jax.experimental.pallas import tpu as pltpu
from jax.sharding import PartitionSpec as P

MESH = pl.DeviceIdType.MESH
BF16 = jnp.bfloat16
F32 = jnp.float32
TERM_ROWS = 16
X_TILE = 256
GRAM_TILE = 256
VMEM_LIMIT = 59 * 1024 * 1024


def one_hot(rows, count):
    at = lax.broadcasted_iota(jnp.int32, (count, rows.shape[1]), 0)
    return jnp.where(at == rows, F32(1.0), F32(0.0)).astype(BF16)


def two_parts(x):
    high = x.astype(BF16)
    low = (x - high.astype(F32)).astype(BF16)
    return jnp.concatenate([high, low], axis=0)


def sum_parts(x):
    half = x.shape[0] // 2
    return x[:half] + x[half:]


def assemble_and_send(
    groups, parts, lam_dev,
    count_ref, refined_ref, rows_ref, coef_ref, modes_ref, owner_ref, factor_hbm,
    dual_ref, coarse_ref,
    factor, picker, weight, stacked, panel, gram, term, terms, turned,
    load_sem, send_dual, recv_dual, send_term, recv_term, send_turn, recv_turn, send_pair, recv_pair, keep_sem,
):
    row = lax.axis_index("row")
    part = lax.axis_index("help")
    core = part % 2
    chip = part // 2
    chips = parts // 2
    slots, order, _ = factor_hbm.shape
    width = rows_ref.shape[1]
    modes = modes_ref.shape[0]
    used = slots * modes
    share = width // parts

    loads = []
    for tile in range(order // X_TILE):
        at = pl.ds(tile * X_TILE, X_TILE)
        loads.append(pltpu.make_async_copy(factor_hbm.at[:, at, :], factor[tile], load_sem.at[tile]))
        loads[-1].start()

    barrier = pltpu.get_barrier_semaphore()

    def greet_help(step, _):
        pl.semaphore_signal(barrier, inc=1, device_id=(row, (part + step) % parts), device_id_type=MESH)
        return 0

    def greet_row(step, _):
        pl.semaphore_signal(barrier, inc=1, device_id=((row + step) % groups, part), device_id_type=MESH)
        return 0

    lax.fori_loop(1, parts, greet_help, 0)
    lax.fori_loop(1, groups, greet_row, 0)

    stacked[...] = jnp.zeros_like(stacked)
    column = lax.broadcasted_iota(jnp.int32, (1, width), 1)
    term_row = lax.broadcasted_iota(jnp.int32, (TERM_ROWS, width), 0)
    for slot in range(slots):
        stacked[slot * modes : (slot + 1) * modes, :] = modes_ref[:, slot, :]
        weight[slot] = jnp.where(column < count_ref[slot], coef_ref[slot : slot + 1, :], F32(0.0))
        picker[slot] = one_hot(rows_ref[slot : slot + 1, :], order)
    both = two_parts(stacked[...])
    total = jnp.zeros((TERM_ROWS, groups * lam_dev), F32)
    for slot in range(slots):
        picked = sum_parts(jnp.dot(both, picker[slot], preferred_element_type=F32))
        mine = (term_row >= slot * modes) & (term_row < (slot + 1) * modes)
        values = jnp.where(mine, picked * weight[slot], F32(0.0))
        owned = one_hot(owner_ref[slot : slot + 1, :], groups * lam_dev)
        total += sum_parts(
            lax.dot_general(two_parts(values), owned, (((1,), (1,)), ((), ())), preferred_element_type=F32)
        )
    term[...] = total.astype(BF16)
    terms[chip] = total.astype(BF16)

    pl.semaphore_wait(barrier, parts - 1 + groups - 1)

    def term_copy(step):
        other = (chip + step) % chips
        return pltpu.make_async_remote_copy(
            src_ref=term, dst_ref=terms.at[chip],
            send_sem=send_term.at[step], recv_sem=recv_term.at[step],
            device_id=(row, other * 2 + core), device_id_type=MESH,
        )

    def term_arrival(step):
        other = (chip + chips - step) % chips
        return pltpu.make_async_remote_copy(
            src_ref=term, dst_ref=terms.at[other],
            send_sem=send_term.at[step], recv_sem=recv_term.at[step],
            device_id=(row, other * 2 + core), device_id_type=MESH,
        )

    def start(copy):
        def body(step, _):
            copy(step).start()
            return 0
        return body

    def arrived(copy):
        def body(step, _):
            copy(step).wait_recv()
            return 0
        return body

    def sent(copy):
        def body(step, _):
            copy(step).wait_send()
            return 0
        return body

    lax.fori_loop(1, chips, start(term_copy), 0)

    chosen = jnp.int32(0)
    for entry in range(refined_ref.shape[1]):
        listed = refined_ref[0, entry]
        chosen = jnp.where(listed == part * slots + 1, jnp.int32(1), chosen)
    scale = weight[chosen]
    for tile in range(order // X_TILE):
        loads[tile].wait()
        at = pl.ds(tile * X_TILE, X_TILE)
        picked = jnp.dot(factor[tile][chosen], picker[chosen], preferred_element_type=F32)
        panel[at, :] = (picked * scale).astype(BF16)
    for tile in range(width // GRAM_TILE):
        at = pl.ds(tile * GRAM_TILE, GRAM_TILE)
        gram[at, :] = lax.dot_general(
            panel[:, at], panel[...], (((0,), (0,)), ((), ())), preferred_element_type=F32
        ).astype(BF16)

    def dual_copy(step):
        other = (part + step) % parts
        return pltpu.make_async_remote_copy(
            src_ref=gram.at[pl.ds(other * share, share), :], dst_ref=dual_ref.at[part],
            send_sem=send_dual.at[step], recv_sem=recv_dual.at[step],
            device_id=(row, other), device_id_type=MESH,
        )

    def dual_arrival(step):
        other = (part + parts - step) % parts
        return pltpu.make_async_remote_copy(
            src_ref=gram.at[pl.ds(other * share, share), :], dst_ref=dual_ref.at[other],
            send_sem=send_dual.at[step], recv_sem=recv_dual.at[step],
            device_id=(row, other), device_id_type=MESH,
        )

    lax.fori_loop(1, parts, start(dual_copy), 0)
    keep_dual = pltpu.make_async_copy(
        gram.at[pl.ds(part * share, share), :], dual_ref.at[part], keep_sem.at[0]
    )
    keep_dual.start()

    lax.fori_loop(1, chips, arrived(term_arrival), 0)
    beside = terms[...].reshape(chips * TERM_ROWS, groups * lam_dev)
    turned[...] = jnp.transpose(beside.astype(F32)).astype(BF16)

    def turn_copy(step):
        other = (row + step) % groups
        return pltpu.make_async_remote_copy(
            src_ref=turned.at[pl.ds(other * lam_dev, lam_dev), :], dst_ref=coarse_ref.at[core, row],
            send_sem=send_turn.at[step], recv_sem=recv_turn.at[step],
            device_id=(other, part), device_id_type=MESH,
        )

    def turn_arrival(step):
        other = (row + groups - step) % groups
        return pltpu.make_async_remote_copy(
            src_ref=turned.at[pl.ds(other * lam_dev, lam_dev), :], dst_ref=coarse_ref.at[core, other],
            send_sem=send_turn.at[step], recv_sem=recv_turn.at[step],
            device_id=(other, part), device_id_type=MESH,
        )

    lax.fori_loop(1, groups, start(turn_copy), 0)
    keep_turn = pltpu.make_async_copy(
        turned.at[pl.ds(row * lam_dev, lam_dev), :], coarse_ref.at[core, row], keep_sem.at[1]
    )
    keep_turn.start()
    keep_turn.wait()
    lax.fori_loop(1, groups, arrived(turn_arrival), 0)

    there = chip * 2 + 1 - core
    pair_copy = pltpu.make_async_remote_copy(
        src_ref=coarse_ref.at[core], dst_ref=coarse_ref.at[core],
        send_sem=send_pair, recv_sem=recv_pair,
        device_id=(row, there), device_id_type=MESH,
    )
    pair_arrival = pltpu.make_async_remote_copy(
        src_ref=coarse_ref.at[1 - core], dst_ref=coarse_ref.at[1 - core],
        send_sem=send_pair, recv_sem=recv_pair,
        device_id=(row, there), device_id_type=MESH,
    )
    pair_copy.start()
    pair_arrival.wait_recv()
    keep_dual.wait()
    lax.fori_loop(1, parts, arrived(dual_arrival), 0)
    pair_copy.wait_send()
    lax.fori_loop(1, chips, sent(term_copy), 0)
    lax.fori_loop(1, groups, sent(turn_copy), 0)
    lax.fori_loop(1, parts, sent(dual_copy), 0)


def put_in_order(slots, used, refined_ref, dual_ref, coarse_ref, blocks_ref, out_ref):
    for entry in range(refined_ref.shape[1]):
        blocks_ref[entry] = dual_ref[lax.div(refined_ref[0, entry], slots)]
    cores, groups, lam_dev, lanes = coarse_ref.shape
    per_group = (lanes // TERM_ROWS) * cores * used
    source = lax.broadcasted_iota(jnp.int32, (cores * lanes, 1), 0)
    core, inside = source // lanes, source % lanes
    chip, at = inside // TERM_ROWS, inside % TERM_ROWS
    target = jnp.where(at < used, (chip * cores + core) * used + at, -512)
    lane = lax.broadcasted_iota(jnp.int32, (cores * lanes, 2 * lanes), 1)
    beside = jnp.concatenate(
        [coarse_ref[c].reshape(groups * lam_dev, lanes) for c in range(cores)], axis=1
    )
    shift = per_group - lanes
    even = jnp.dot(beside, jnp.where(lane == target, F32(1.0), F32(0.0)).astype(BF16), preferred_element_type=F32)
    odd = jnp.dot(beside, jnp.where(lane == target + shift, F32(1.0), F32(0.0)).astype(BF16), preferred_element_type=F32)
    for pair in range(groups // 2):
        first = even[2 * pair * lam_dev : (2 * pair + 1) * lam_dev]
        second = odd[(2 * pair + 1) * lam_dev : (2 * pair + 2) * lam_dev]
        base = pair * 3 * lanes
        out_ref[:, base : base + lanes] = first[:, :lanes]
        out_ref[:, base + lanes : base + 2 * lanes] = first[:, lanes:] + second[:, :lanes]
        out_ref[:, base + 2 * lanes : base + 3 * lanes] = second[:, lanes:]


def on_device(groups, parts, factor_inv, b_rows, b_coef, b_count, refined, modes, owner, lam_dev):
    slots, order, _ = factor_inv.shape
    width = b_rows.shape[1]
    mode_count = modes.shape[1]
    share = width // parts
    chips = parts // 2
    lanes = chips * TERM_ROWS
    lam = groups * lam_dev
    vmem = pl.BlockSpec(memory_space=pltpu.VMEM)
    smem = pl.BlockSpec(memory_space=pltpu.SMEM)
    anywhere = pl.BlockSpec(memory_space=pl.ANY)
    dual, coarse = pl.pallas_call(
        functools.partial(assemble_and_send, groups, parts, lam_dev),
        out_shape=(
            jax.ShapeDtypeStruct((parts, share, width), BF16),
            jax.ShapeDtypeStruct((2, groups, lam_dev, lanes), BF16),
        ),
        in_specs=[smem, smem, vmem, vmem, vmem, vmem, anywhere],
        out_specs=(anywhere, anywhere),
        scratch_shapes=[
            [pltpu.VMEM((slots, X_TILE, order), BF16) for _ in range(order // X_TILE)],
            pltpu.VMEM((slots, order, width), BF16),
            pltpu.VMEM((slots, 1, width), F32),
            pltpu.VMEM((TERM_ROWS, order), F32),
            pltpu.VMEM((order, width), BF16),
            pltpu.VMEM((width, width), BF16),
            pltpu.VMEM((TERM_ROWS, lam), BF16),
            pltpu.VMEM((chips, TERM_ROWS, lam), BF16),
            pltpu.VMEM((lam, lanes), BF16),
            pltpu.SemaphoreType.DMA((order // X_TILE,)),
            pltpu.SemaphoreType.DMA((parts,)),
            pltpu.SemaphoreType.DMA((parts,)),
            pltpu.SemaphoreType.DMA((chips,)),
            pltpu.SemaphoreType.DMA((chips,)),
            pltpu.SemaphoreType.DMA((groups,)),
            pltpu.SemaphoreType.DMA((groups,)),
            pltpu.SemaphoreType.DMA,
            pltpu.SemaphoreType.DMA,
            pltpu.SemaphoreType.DMA((2,)),
        ],
        compiler_params=pltpu.CompilerParams(
            collective_id=0, has_side_effects=True, vmem_limit_bytes=VMEM_LIMIT
        ),
        name="assemble_and_send",
    )(b_count, refined, b_rows, b_coef, jnp.transpose(modes, (1, 0, 2)), owner, factor_inv)
    blocks, turned = pl.pallas_call(
        functools.partial(put_in_order, slots, slots * mode_count),
        out_shape=(
            jax.ShapeDtypeStruct((refined.shape[1], share, width), BF16),
            jax.ShapeDtypeStruct((lam_dev, groups * parts * slots * mode_count), F32),
        ),
        in_specs=[smem, vmem, vmem],
        out_specs=(vmem, vmem),
        compiler_params=pltpu.CompilerParams(vmem_limit_bytes=16 * 1024 * 1024),
        name="put_in_order",
    )(refined, dual, coarse)
    return blocks, turned.T


def solution(mesh):
    groups, parts = mesh.shape["row"], mesh.shape["help"]
    lam_dev = 16
    in_specs = (
        P(("row", "help"), None, None),
        P(("row", "help"), None),
        P(("row", "help"), None),
        P(("row", "help")),
        P("row", None),
        P(("row", "help"), None, None),
        P(("row", "help"), None),
    )
    out_specs = (P("row", "help", None), P(None, "row"))

    def body(*args):
        return on_device(groups, parts, *args, lam_dev)

    return jax.shard_map(body, mesh=mesh, in_specs=in_specs, out_specs=out_specs, check_vma=False)
```

time: 169 us -> 40.8 us (0.24)
  local copies, waits for them, and re-layouts: 86 us -> 1.99 us
  Pallas kernels: 0 us -> 37.9 us
  blocking collectives: 27.3 us -> 0 us
  waiting for transfers between devices: 26.7 us -> 0 us
  starting transfers between devices: 13.5 us -> 0 us
  other arithmetic: 11.6 us -> 0 us
  matrix products: 1.92 us -> 0 us
    gather x6 -> x0, local copies, waits for them, and re-layouts: 68.3 us -> none  [the longest x3 59.6 us: on_device(): jnp.take_along_axis(modes, gather_rows, axis=2) * weights[:, None, :]]
    pallas_call x0 -> x2, Pallas kernels: none -> 37.9 us  [the longest x1 36.3 us: on_device(): pl.pallas_call(functools.partial(assemble_and_send, groups, parts, lam_de...]
    all_gather x1 -> x0, blocking collectives: 27.3 us -> none  [on_device(): grouped = lax.all_gather(term, 'help', axis=0, tiled=True)]
    all_to_all x2 -> x0, waiting for transfers between devices: 26.7 us -> none  [the longest x1 26.7 us: on_device(): lax.all_to_all(stacked, 'help', split_axis=1, concat_axis=1, tiled=True)]
    all_to_all x2 -> x0, starting transfers between devices: 13.5 us -> none  [the longest x1 9.67 us: on_device(): lax.all_to_all(grouped, 'row', split_axis=1, concat_axis=0, tiled=True)]
    unnamed x4 -> x0, other arithmetic: 7.64 us -> none
    all_to_all x5 -> x0, local copies, waits for them, and re-layouts: 5.85 us -> none  [the longest x4 5.75 us: on_device(): lax.all_to_all(grouped, 'row', split_axis=1, concat_axis=0, tiled=True)]
    unnamed x18 -> x6, local copies, waits for them, and re-layouts: 7.03 us -> 1.99 us
  transfers between devices with their start and end apart: 2 -> 0, of which waited for: 1 -> 0; matrix products, arithmetic and copies ran while one was open for 13% -> 0% of each run, Pallas kernels for 0% -> 0%
where the time goes in v1:
time: 40.8 us; the launch traced here: 40.6 us
  Pallas kernels  37.9 us (93%)
  local copies, waits for them, and re-layouts  1.99 us (5%)
  between operations  0.67 us (2%)
    pallas_call x1, Pallas kernels, on_device(): pl.pallas_call(functools.partial(assemble_and_send, groups, parts, lam_de...  36.3 us
    unnamed x6, local copies, waits for them, and re-layouts  1.99 us
    pallas_call x1, Pallas kernels, on_device(): pl.pallas_call(functools.partial(put_in_order, slots, slots * mode_count)...  1.65 us

profile of v1, /device:TPU:1, one launch (start us, length us, event | category | flops | bytes accessed | tf_op | source)
XLA Modules:
  0.0 40.6 jit_solution(9520501955556174854)
XLA Ops:
  0.6 0.0 copy-start.2
  0.6 36.3 %assemble_and_send.1 = (bf16[16,32,512]{2,1,0:T(8,128)(2,1)}, bf16[2,32,16,128]{3,2,1,0:T(8,128)(2,1)}) custom-call(s32[2]{0:T(128)} %count_ref.1, s32[1,8]{1,0:T(1,128)} %refined_ref.3, s32[2,512]{1,0:T(2,128)} %rows_ref.1, f32[2,512]{1,0:T(2,128)} %coef_ref.1, f32[6,2,1024]{2,1,0:T(2,128)} %bitcast.2, s32[2,512]{1,0:T(2,128)} %owner_ref.1, ...), custom_call_target="tpu_custom_call" | custom-call | tf_op jit(solution)/shard_map/assemble_and_send/pallas_call | solution.py:253
  36.9 0.0 copy-done.2
  36.9 0.0 copy-start
  37.0 1.0 %copy-done = bf16[16,32,512]{2,1,0:T(8,128)(2,1)S(1)} copy-done((bf16[16,32,512]{2,1,0:T(8,128)(2,1)S(1)}, bf16[16,32,512]{2,1,0:T(8,128)(2,1)}, u32[]{:S(2)}) %copy-start) | copy-done | bytes 524312
  38.0 0.0 copy-start.1
  38.0 0.9 %copy-done.1 = bf16[2,32,16,128]{3,2,1,0:T(8,128)(2,1)S(1)} copy-done((bf16[2,32,16,128]{3,2,1,0:T(8,128)(2,1)S(1)}, bf16[2,32,16,128]{3,2,1,0:T(8,128)(2,1)}, u32[]{:S(2)}) %copy-start.1) | copy-done | bytes 262168
  38.9 1.6 %put_in_order.1 = (bf16[8,32,512]{2,1,0:T(8,128)(2,1)}, f32[16,6144]{1,0:T(8,128)}) custom-call(s32[1,8]{1,0:T(1,128)S(1)} %copy-done.2, bf16[16,32,512]{2,1,0:T(8,128)(2,1)S(1)} %copy-done, bf16[2,32,16,128]{3,2,1,0:T(8,128)(2,1)S(1)} %copy-done.1), custom_call_target="tpu_custom_call" | custom-call | tf_op jit(solution)/shard_map/put_in_order/pallas_call | solution.py:287
Async XLA Ops:
  0.6 36.3 %copy-start.2 = (s32[1,8]{1,0:T(1,128)S(1)}, s32[1,8]{1,0:T(1,128)}, u32[]{:S(2)}) copy-start(s32[1,8]{1,0:T(1,128)} %refined_ref.3) | copy-start | bytes 100
  36.9 1.0 %copy-start = (bf16[16,32,512]{2,1,0:T(8,128)(2,1)S(1)}, bf16[16,32,512]{2,1,0:T(8,128)(2,1)}, u32[]{:S(2)}) copy-start(bf16[16,32,512]{2,1,0:T(8,128)(2,1)} %get-tuple-element.6.dual_ref) | copy-start | bytes 1572868
  38.0 0.9 %copy-start.1 = (bf16[2,32,16,128]{3,2,1,0:T(8,128)(2,1)S(1)}, bf16[2,32,16,128]{3,2,1,0:T(8,128)(2,1)}, u32[]{:S(2)}) copy-start(bf16[2,32,16,128]{3,2,1,0:T(8,128)(2,1)} %get-tuple-element.7.coarse_ref) | copy-start | bytes 786436

commit v2 on v1

v2 whole, which is shorter than its diff:
```python
import functools

import jax
import jax.numpy as jnp
from jax import lax
from jax.experimental import pallas as pl
from jax.experimental.pallas import tpu as pltpu
from jax.sharding import PartitionSpec as P

MESH = pl.DeviceIdType.MESH
BF16 = jnp.bfloat16
F32 = jnp.float32
SLOT_ROWS = 8
LANES = 128
X_TILE = 256
GRAM_TILE = 256
VMEM_LIMIT = 28 * 1024 * 1024
ROW_X = 4


def one_hot(rows, count):
    at = lax.broadcasted_iota(jnp.int32, (count, rows.shape[1]), 0)
    return jnp.where(at == rows, F32(1.0), F32(0.0)).astype(BF16)


def two_parts(x):
    high = x.astype(BF16)
    low = (x - high.astype(F32)).astype(BF16)
    return jnp.concatenate([high, low], axis=0)


def sum_parts(x):
    half = x.shape[0] // 2
    return x[:half] + x[half:]


def ring_distance(step, size):
    return min(step, size - step)


def far_first(steps, sizes):
    def way(step):
        return -sum(ring_distance(a, n) for a, n in zip(step, sizes))
    return sorted((step for step in steps if any(step)), key=way)


def pick_lanes(table, rows):
    height, order = table.shape
    pieces = []
    for piece in range(rows.shape[1] // LANES):
        index = jnp.broadcast_to(rows[:, piece * LANES : (piece + 1) * LANES], (height, LANES))
        block, lane = lax.shift_right_logical(index, 7), lax.bitwise_and(index, LANES - 1)
        found = jnp.zeros((height, LANES), table.dtype)
        for source in range(order // LANES):
            values = jnp.take_along_axis(
                table[:, source * LANES : (source + 1) * LANES], lane, axis=1, mode="promise_in_bounds"
            )
            found = jnp.where(block == source, values, found)
        pieces.append(found)
    return jnp.concatenate(pieces, axis=1)


def assemble_and_send(
    groups, parts, lam_dev,
    count_hbm, refined_hbm, rows_hbm, coef_hbm, modes_hbm, owner_hbm, factor_hbm,
    blocks_ref, ordered_ref,
    count_ref, refined_ref, rows_ref, coef_ref, modes_ref, owner_ref,
    factor, picker, weight, stacked, panel, gram, term, terms, turned, coarse_ref, dual_ref,
    small_sem, load_sem, send_dual, recv_dual, send_term, recv_term, send_turn, recv_turn, send_pair, recv_pair, row_ready,
):
    row = lax.axis_index("row")
    part = lax.axis_index("help")
    core = part % 2
    chip = part // 2
    chips = parts // 2
    slots, order, _ = factor_hbm.shape
    width = rows_ref.shape[1]
    modes = modes_ref.shape[0]
    lam = groups * lam_dev
    share = width // parts

    small = [
        pltpu.make_async_copy(source, target, small_sem.at[number])
        for number, (source, target) in enumerate((
            (rows_hbm, rows_ref), (owner_hbm, owner_ref), (modes_hbm, modes_ref), (coef_hbm, coef_ref),
            (count_hbm, count_ref), (refined_hbm, refined_ref),
        ))
    ]
    for copy in small:
        copy.start()
    loads = []
    for tile in range(order // X_TILE):
        at = pl.ds(tile * X_TILE, X_TILE)
        loads.append(pltpu.make_async_copy(factor_hbm.at[:, at, :], factor[tile], load_sem.at[tile]))
        loads[-1].start()

    barrier = pltpu.get_barrier_semaphore()

    def greet_help(step, _):
        pl.semaphore_signal(barrier, inc=1, device_id=(row, (part + step) % parts), device_id_type=MESH)
        return 0

    head = groups // 2

    @pl.when(row != head)
    def _():
        pl.semaphore_signal(barrier, inc=1, device_id=(head, part), device_id_type=MESH)

    lax.fori_loop(1, parts, greet_help, 0)

    stacked[...] = jnp.zeros_like(stacked)
    column = lax.broadcasted_iota(jnp.int32, (1, width), 1)
    for copy in small:
        copy.wait()
    for slot in range(slots):
        stacked[slot * SLOT_ROWS : slot * SLOT_ROWS + modes, :] = modes_ref[:, slot, :]
        weight[slot] = jnp.where(column < count_ref[slot], coef_ref[slot : slot + 1, :], F32(0.0))
    totals = []
    for slot in range(slots):
        table = stacked[slot * SLOT_ROWS : (slot + 1) * SLOT_ROWS, :]
        values = pick_lanes(table, rows_ref[slot : slot + 1, :]) * weight[slot]
        owned = one_hot(owner_ref[slot : slot + 1, :], lam)
        totals.append(sum_parts(
            lax.dot_general(two_parts(values), owned, (((1,), (1,)), ((), ())), preferred_element_type=F32)
        ))
    total = jnp.concatenate(totals, axis=0).astype(BF16)
    term[...] = total
    terms[chip] = total

    def start(copy):
        def body(step, _):
            copy(step).start()
            return 0
        return body

    def arrived(copy):
        def body(step, _):
            copy(step).wait_recv()
            return 0
        return body

    def sent(copy):
        def body(step, _):
            copy(step).wait_send()
            return 0
        return body

    def term_copy(step):
        other = (chip + step) % chips
        return pltpu.make_async_remote_copy(
            src_ref=term, dst_ref=terms.at[chip],
            send_sem=send_term.at[step], recv_sem=recv_term.at[step],
            device_id=(row, other * 2 + core), device_id_type=MESH,
        )

    def term_arrival(step):
        other = (chip + chips - step) % chips
        return pltpu.make_async_remote_copy(
            src_ref=term, dst_ref=terms.at[other],
            send_sem=send_term.at[step], recv_sem=recv_term.at[step],
            device_id=(row, other * 2 + core), device_id_type=MESH,
        )

    def row_is_here(step, _):
        pl.semaphore_signal(row_ready, inc=1, device_id=((row + step) % groups, part), device_id_type=MESH)
        return 0

    def meet_and_send_terms():
        pl.semaphore_wait(barrier, parts - 1 + jnp.where(row == head, groups - 1, 0))

        @pl.when(row == head)
        def _():
            lax.fori_loop(1, groups, row_is_here, 0)

        for (step,) in far_first([(z,) for z in range(chips)], (chips,)):
            term_copy(step).start()

    late = chip >= chips // 2

    @pl.when(late)
    def _():
        meet_and_send_terms()

    chosen = jnp.int32(0)
    for entry in range(refined_ref.shape[1]):
        listed = refined_ref[0, entry]
        chosen = jnp.where(listed == part * slots + 1, jnp.int32(1), chosen)
    rows_here = jnp.where(chosen == 1, rows_ref[1:2, :], rows_ref[0:1, :])
    picker[...] = one_hot(rows_here, order)
    scale = weight[chosen]
    for tile in range(order // X_TILE):
        loads[tile].wait()
        picked = jnp.dot(factor[tile][chosen], picker[...], preferred_element_type=F32)
        panel[pl.ds(tile * X_TILE, X_TILE), :] = (picked * scale).astype(BF16)
    for tile in range(width // GRAM_TILE):
        at = pl.ds(tile * GRAM_TILE, GRAM_TILE)
        gram[at, :] = lax.dot_general(
            panel[:, at], panel[...], (((0,), (0,)), ((), ())), preferred_element_type=F32
        ).astype(BF16)

    def dual_copy(step):
        other = (chip + step // 2) % chips * 2 + (core + step % 2) % 2
        return pltpu.make_async_remote_copy(
            src_ref=gram.at[pl.ds(other * share, share), :], dst_ref=dual_ref.at[part],
            send_sem=send_dual.at[step], recv_sem=recv_dual.at[step],
            device_id=(row, other), device_id_type=MESH,
        )

    def dual_arrival(step):
        other = (chip + chips - step // 2) % chips * 2 + (core + step % 2) % 2
        return pltpu.make_async_remote_copy(
            src_ref=gram.at[pl.ds(other * share, share), :], dst_ref=dual_ref.at[other],
            send_sem=send_dual.at[step], recv_sem=recv_dual.at[step],
            device_id=(row, other), device_id_type=MESH,
        )

    @pl.when(jnp.logical_not(late))
    def _():
        meet_and_send_terms()

    for z, other_core in far_first([(z, c) for z in range(chips) for c in range(2)], (chips, 2)):
        dual_copy(2 * z + other_core).start()
    dual_ref[part] = gram[pl.ds(part * share, share), :]

    lax.fori_loop(1, chips, arrived(term_arrival), 0)
    lanes = chips * slots * SLOT_ROWS
    beside = terms[...].reshape(lanes, lam)
    turned[...] = jnp.transpose(beside.astype(F32)).astype(BF16)

    y, x = row // ROW_X, row % ROW_X
    row_y = groups // ROW_X

    def turn_copy(step):
        other = (y + step // ROW_X) % row_y * ROW_X + (x + step % ROW_X) % ROW_X
        return pltpu.make_async_remote_copy(
            src_ref=turned.at[pl.ds(other * lam_dev, lam_dev), :], dst_ref=coarse_ref.at[core, row],
            send_sem=send_turn.at[step], recv_sem=recv_turn.at[step],
            device_id=(other, part), device_id_type=MESH,
        )

    def turn_arrival(step):
        other = (y + row_y - step // ROW_X) % row_y * ROW_X + (x + ROW_X - step % ROW_X) % ROW_X
        return pltpu.make_async_remote_copy(
            src_ref=turned.at[pl.ds(other * lam_dev, lam_dev), :], dst_ref=coarse_ref.at[core, other],
            send_sem=send_turn.at[step], recv_sem=recv_turn.at[step],
            device_id=(other, part), device_id_type=MESH,
        )

    @pl.when(row != head)
    def _():
        pl.semaphore_wait(row_ready, 1)

    for step_y, step_x in far_first([(a, b) for a in range(row_y) for b in range(ROW_X)], (row_y, ROW_X)):
        turn_copy(ROW_X * step_y + step_x).start()
    coarse_ref[core, row] = turned[pl.ds(row * lam_dev, lam_dev), :]

    source = lax.broadcasted_iota(jnp.int32, (2 * lanes, 1), 0)
    from_core, inside = source // lanes, source % lanes
    from_chip, at = inside // (slots * SLOT_ROWS), inside % (slots * SLOT_ROWS)
    from_slot, mode = at // SLOT_ROWS, at % SLOT_ROWS
    target = jnp.where(mode < modes, ((from_chip * 2 + from_core) * slots + from_slot) * modes + mode, -512)
    lane = lax.broadcasted_iota(jnp.int32, (2 * lanes, 2 * lanes), 1)
    shift = parts * slots * modes - lanes
    to_even = jnp.where(lane == target, F32(1.0), F32(0.0)).astype(BF16)
    to_odd = jnp.where(lane == target + shift, F32(1.0), F32(0.0)).astype(BF16)

    lax.fori_loop(1, groups, arrived(turn_arrival), 0)

    there = chip * 2 + 1 - core
    pair_copy = pltpu.make_async_remote_copy(
        src_ref=coarse_ref.at[core], dst_ref=coarse_ref.at[core],
        send_sem=send_pair, recv_sem=recv_pair,
        device_id=(row, there), device_id_type=MESH,
    )
    pair_arrival = pltpu.make_async_remote_copy(
        src_ref=coarse_ref.at[1 - core], dst_ref=coarse_ref.at[1 - core],
        send_sem=send_pair, recv_sem=recv_pair,
        device_id=(row, there), device_id_type=MESH,
    )
    pair_copy.start()
    pair_arrival.wait_recv()
    halves = jnp.concatenate([coarse_ref[c].reshape(groups * lam_dev, lanes) for c in range(2)], axis=1)
    even = jnp.dot(halves, to_even, preferred_element_type=F32)
    odd = jnp.dot(halves, to_odd, preferred_element_type=F32)
    for pair in range(groups // 2):
        first = even[2 * pair * lam_dev : (2 * pair + 1) * lam_dev]
        second = odd[(2 * pair + 1) * lam_dev : (2 * pair + 2) * lam_dev]
        base = pair * 3 * lanes
        ordered_ref[:, base : base + lanes] = first[:, :lanes]
        ordered_ref[:, base + lanes : base + 2 * lanes] = first[:, lanes:] + second[:, :lanes]
        ordered_ref[:, base + 2 * lanes : base + 3 * lanes] = second[:, lanes:]

    pair_copy.wait_send()
    lax.fori_loop(1, chips, sent(term_copy), 0)
    lax.fori_loop(1, groups, sent(turn_copy), 0)
    lax.fori_loop(1, parts, sent(dual_copy), 0)
    lax.fori_loop(1, parts, arrived(dual_arrival), 0)
    for entry in range(refined_ref.shape[1]):
        blocks_ref[entry] = dual_ref[lax.shift_right_logical(refined_ref[0, entry], slots - 1)]


def on_device(groups, parts, factor_inv, b_rows, b_coef, b_count, refined, modes, owner, lam_dev):
    slots, order, _ = factor_inv.shape
    width = b_rows.shape[1]
    mode_count = modes.shape[1]
    share = width // parts
    chips = parts // 2
    rows = slots * SLOT_ROWS
    lanes = chips * rows
    lam = groups * lam_dev
    columns = groups * parts * slots * mode_count
    vmem = pl.BlockSpec(memory_space=pltpu.VMEM)
    anywhere = pl.BlockSpec(memory_space=pl.ANY)
    inputs = (b_count, refined, b_rows, b_coef, jnp.transpose(modes, (1, 0, 2)), owner, factor_inv)
    blocks, ordered = pl.pallas_call(
        functools.partial(assemble_and_send, groups, parts, lam_dev),
        out_shape=(
            pltpu.VMEM((refined.shape[1], share, width), BF16),
            pltpu.VMEM((lam_dev, columns), F32),
        ),
        in_specs=[anywhere] * 7,
        out_specs=(vmem, vmem),
        scratch_shapes=[
            pltpu.SMEM(b_count.shape, jnp.int32),
            pltpu.SMEM(refined.shape, jnp.int32),
            pltpu.VMEM(b_rows.shape, jnp.int32),
            pltpu.VMEM(b_coef.shape, F32),
            pltpu.VMEM((mode_count, slots, order), F32),
            pltpu.VMEM(owner.shape, jnp.int32),
            [pltpu.VMEM((slots, X_TILE, order), BF16) for _ in range(order // X_TILE)],
            pltpu.VMEM((order, width), BF16),
            pltpu.VMEM((slots, 1, width), F32),
            pltpu.VMEM((rows, order), F32),
            pltpu.VMEM((order, width), BF16),
            pltpu.VMEM((width, width), BF16),
            pltpu.VMEM((rows, lam), BF16),
            pltpu.VMEM((chips, rows, lam), BF16),
            pltpu.VMEM((lam, lanes), BF16),
            pltpu.VMEM((2, groups, lam_dev, lanes), BF16),
            pltpu.VMEM((parts, share, width), BF16),
            pltpu.SemaphoreType.DMA((6,)),
            pltpu.SemaphoreType.DMA((order // X_TILE,)),
            pltpu.SemaphoreType.DMA((parts,)),
            pltpu.SemaphoreType.DMA((parts,)),
            pltpu.SemaphoreType.DMA((chips,)),
            pltpu.SemaphoreType.DMA((chips,)),
            pltpu.SemaphoreType.DMA((groups,)),
            pltpu.SemaphoreType.DMA((groups,)),
            pltpu.SemaphoreType.DMA,
            pltpu.SemaphoreType.DMA,
            pltpu.SemaphoreType.REGULAR,
        ],
        compiler_params=pltpu.CompilerParams(
            collective_id=0, has_side_effects=True, vmem_limit_bytes=VMEM_LIMIT
        ),
        name="assemble_and_send",
    )(*(pltpu.with_memory_space_constraint(array, pltpu.HBM) for array in inputs))
    return blocks, ordered.T


def solution(mesh):
    groups, parts = mesh.shape["row"], mesh.shape["help"]
    lam_dev = 16
    in_specs = (
        P(("row", "help"), None, None),
        P(("row", "help"), None),
        P(("row", "help"), None),
        P(("row", "help")),
        P("row", None),
        P(("row", "help"), None, None),
        P(("row", "help"), None),
    )
    out_specs = (P("row", "help", None), P(None, "row"))

    def body(*args):
        return on_device(groups, parts, *args, lam_dev)

    return jax.shard_map(body, mesh=mesh, in_specs=in_specs, out_specs=out_specs, check_vma=False)
```

time: 40.8 us -> 32.9 us (0.81)
  Pallas kernels: 37.9 us -> 30.6 us
  local copies, waits for them, and re-layouts: 1.99 us -> 1.45 us
    pallas_call x1, Pallas kernels: 36.3 us -> 30.6 us  [on_device(): pl.pallas_call(functools.partial(assemble_and_send, groups, parts, lam_de...]
    pallas_call x1 -> x0, Pallas kernels: 1.65 us -> none  [on_device(): pl.pallas_call(functools.partial(put_in_order, slots, slots * mode_count)...]
    unnamed x6 -> x2, local copies, waits for them, and re-layouts: 1.99 us -> 1.45 us
where the time goes in v2:
time: 32.9 us; the launch traced here: 32.7 us
  Pallas kernels  30.6 us (93%)
  local copies, waits for them, and re-layouts  1.45 us (4%)
  between operations  0.64 us (2%)
    pallas_call x1, Pallas kernels, on_device(): pl.pallas_call(functools.partial(assemble_and_send, groups, parts, lam_de...  30.6 us
    unnamed x2, local copies, waits for them, and re-layouts  1.45 us

profile of v2, /device:TPU:1, one launch (start us, length us, event | category | flops | bytes accessed | tf_op | source)
XLA Modules:
  0.0 32.7 jit_solution(12583819184399530949)
XLA Ops:
  0.6 30.6 %assemble_and_send.1 = (bf16[8,32,512]{2,1,0:T(8,128)(2,1)S(1)}, f32[16,6144]{1,0:T(8,128)S(1)}) custom-call(s32[2]{0:T(128)} %count_hbm.1, s32[1,8]{1,0:T(1,128)} %refined_hbm.1, s32[2,512]{1,0:T(2,128)} %rows_hbm.1, f32[2,512]{1,0:T(2,128)} %coef_hbm.1, f32[6,2,1024]{2,1,0:T(2,128)} %bitcast.3, s32[2,512]{1,0:T(2,128)} %owner_hbm.1, ...), custom_call_target="tpu_custom_call" | custom-call | tf_op jit(solution)/shard_map/assemble_and_send/pallas_call | solution.py:315
  31.3 0.7 %copy.11 = bf16[8,32,512]{2,1,0:T(8,128)(2,1)} copy(bf16[8,32,512]{2,1,0:T(8,128)(2,1)S(1)} %get-tuple-element.6) | data formatting | bytes 524288
  32.0 0.7 %copy.12 = f32[6144,16]{0,1:T(8,128)} copy(f32[6144,16]{0,1:T(8,128)S(1)} %bitcast.2) | data formatting | bytes 786432

commit v3 on v2

--- a/solution.py
+++ b/solution.py
@@ -42,6 +42,14 @@
     def way(step):
         return -sum(ring_distance(a, n) for a, n in zip(step, sizes))
     return sorted((step for step in steps if any(step)), key=way)
+
+
+def owner_place(owner, x, lam_dev, column_share):
+    shift = lam_dev.bit_length() - 1
+    holder = lax.shift_right_logical(owner, shift)
+    place = lax.bitwise_and(x + 2 - lax.bitwise_and(holder, ROW_X - 1), ROW_X - 1)
+    holder_y = lax.shift_right_logical(holder, ROW_X.bit_length() - 1)
+    return place * column_share + holder_y * lam_dev + lax.bitwise_and(owner, lam_dev - 1)
 
 
 def pick_lanes(table, rows):
@@ -78,6 +86,10 @@
     modes = modes_ref.shape[0]
     lam = groups * lam_dev
     share = width // parts
+    y, x = row // ROW_X, row % ROW_X
+    row_y = groups // ROW_X
+    column_share = row_y * lam_dev
+    half_width = lam // 2
 
     small = [
         pltpu.make_async_copy(source, target, small_sem.at[number])
@@ -119,7 +131,7 @@
     for slot in range(slots):
         table = stacked[slot * SLOT_ROWS : (slot + 1) * SLOT_ROWS, :]
         values = pick_lanes(table, rows_ref[slot : slot + 1, :]) * weight[slot]
-        owned = one_hot(owner_ref[slot : slot + 1, :], lam)
+        owned = one_hot(owner_place(owner_ref[slot : slot + 1, :], x, lam_dev, column_share), lam)
         totals.append(sum_parts(
             lax.dot_general(two_parts(values), owned, (((1,), (1,)), ((), ())), preferred_element_type=F32)
         ))
@@ -146,17 +158,19 @@
         return body
 
     def term_copy(step):
-        other = (chip + step) % chips
-        return pltpu.make_async_remote_copy(
-            src_ref=term, dst_ref=terms.at[chip],
+        other = (chip + step % chips) % chips
+        at = pl.ds(pl.multiple_of(step // chips * half_width, half_width), half_width)
+        return pltpu.make_async_remote_copy(
+            src_ref=term.at[:, at], dst_ref=terms.at[chip, :, at],
             send_sem=send_term.at[step], recv_sem=recv_term.at[step],
             device_id=(row, other * 2 + core), device_id_type=MESH,
         )
 
     def term_arrival(step):
-        other = (chip + chips - step) % chips
-        return pltpu.make_async_remote_copy(
-            src_ref=term, dst_ref=terms.at[other],
+        other = (chip + chips - step % chips) % chips
+        at = pl.ds(pl.multiple_of(step // chips * half_width, half_width), half_width)
+        return pltpu.make_async_remote_copy(
+            src_ref=term.at[:, at], dst_ref=terms.at[other, :, at],
             send_sem=send_term.at[step], recv_sem=recv_term.at[step],
             device_id=(row, other * 2 + core), device_id_type=MESH,
         )
@@ -172,8 +186,9 @@
         def _():
             lax.fori_loop(1, groups, row_is_here, 0)
 
-        for (step,) in far_first([(z,) for z in range(chips)], (chips,)):
-            term_copy(step).start()
+        for half in range(2):
+            for (step,) in far_first([(z,) for z in range(chips)], (chips,)):
+                term_copy(half * chips + step).start()
 
     late = chip >= chips // 2
 
@@ -222,37 +237,39 @@
         dual_copy(2 * z + other_core).start()
     dual_ref[part] = gram[pl.ds(part * share, share), :]
 
-    lax.fori_loop(1, chips, arrived(term_arrival), 0)
     lanes = chips * slots * SLOT_ROWS
-    beside = terms[...].reshape(lanes, lam)
-    turned[...] = jnp.transpose(beside.astype(F32)).astype(BF16)
-
-    y, x = row // ROW_X, row % ROW_X
-    row_y = groups // ROW_X
 
     def turn_copy(step):
-        other = (y + step // ROW_X) % row_y * ROW_X + (x + step % ROW_X) % ROW_X
-        return pltpu.make_async_remote_copy(
-            src_ref=turned.at[pl.ds(other * lam_dev, lam_dev), :], dst_ref=coarse_ref.at[core, row],
+        other_y, other_x = (y + step // ROW_X) % row_y, (x + step % ROW_X) % ROW_X
+        start_row = (ROW_X + 2 - step % ROW_X) % ROW_X * column_share + other_y * lam_dev
+        return pltpu.make_async_remote_copy(
+            src_ref=turned.at[pl.ds(pl.multiple_of(start_row, lam_dev), lam_dev), :],
+            dst_ref=coarse_ref.at[core, x * row_y + y],
             send_sem=send_turn.at[step], recv_sem=recv_turn.at[step],
-            device_id=(other, part), device_id_type=MESH,
+            device_id=(other_y * ROW_X + other_x, part), device_id_type=MESH,
         )
 
     def turn_arrival(step):
-        other = (y + row_y - step // ROW_X) % row_y * ROW_X + (x + ROW_X - step % ROW_X) % ROW_X
-        return pltpu.make_async_remote_copy(
-            src_ref=turned.at[pl.ds(other * lam_dev, lam_dev), :], dst_ref=coarse_ref.at[core, other],
+        other_y, other_x = (y + row_y - step // ROW_X) % row_y, (x + ROW_X - step % ROW_X) % ROW_X
+        return pltpu.make_async_remote_copy(
+            src_ref=turned.at[pl.ds(0, lam_dev), :], dst_ref=coarse_ref.at[core, other_x * row_y + other_y],
             send_sem=send_turn.at[step], recv_sem=recv_turn.at[step],
-            device_id=(other, part), device_id_type=MESH,
+            device_id=(other_y * ROW_X + other_x, part), device_id_type=MESH,
         )
 
     @pl.when(row != head)
     def _():
         pl.semaphore_wait(row_ready, 1)
 
-    for step_y, step_x in far_first([(a, b) for a in range(row_y) for b in range(ROW_X)], (row_y, ROW_X)):
-        turn_copy(ROW_X * step_y + step_x).start()
-    coarse_ref[core, row] = turned[pl.ds(row * lam_dev, lam_dev), :]
+    halves_of_x = ((2, 1), (0, 3))
+    for half, steps_x in enumerate(halves_of_x):
+        lax.fori_loop(half * chips + 1, (half + 1) * chips, arrived(term_arrival), 0)
+        at = slice(half * half_width, (half + 1) * half_width)
+        beside = terms[:, :, at].reshape(lanes, half_width)
+        turned[at, :] = jnp.transpose(beside.astype(F32)).astype(BF16)
+        for step_y, step_x in far_first([(a, b) for a in range(row_y) for b in steps_x], (row_y, ROW_X)):
+            turn_copy(ROW_X * step_y + step_x).start()
+    coarse_ref[core, x * row_y + y] = turned[pl.ds(2 * column_share + y * lam_dev, lam_dev), :]
 
     source = lax.broadcasted_iota(jnp.int32, (2 * lanes, 1), 0)
     from_core, inside = source // lanes, source % lanes
@@ -264,39 +281,58 @@
     to_even = jnp.where(lane == target, F32(1.0), F32(0.0)).astype(BF16)
     to_odd = jnp.where(lane == target + shift, F32(1.0), F32(0.0)).astype(BF16)
 
-    lax.fori_loop(1, groups, arrived(turn_arrival), 0)
-
     there = chip * 2 + 1 - core
-    pair_copy = pltpu.make_async_remote_copy(
-        src_ref=coarse_ref.at[core], dst_ref=coarse_ref.at[core],
-        send_sem=send_pair, recv_sem=recv_pair,
-        device_id=(row, there), device_id_type=MESH,
-    )
-    pair_arrival = pltpu.make_async_remote_copy(
-        src_ref=coarse_ref.at[1 - core], dst_ref=coarse_ref.at[1 - core],
-        send_sem=send_pair, recv_sem=recv_pair,
-        device_id=(row, there), device_id_type=MESH,
-    )
-    pair_copy.start()
-    pair_arrival.wait_recv()
+
+    def pair_copy(step_x, half):
+        at = pl.ds((x + ROW_X - step_x) % ROW_X * row_y, row_y)
+        return pltpu.make_async_remote_copy(
+            src_ref=coarse_ref.at[half, at], dst_ref=coarse_ref.at[half, at],
+            send_sem=send_pair.at[step_x], recv_sem=recv_pair.at[step_x],
+            device_id=(row, there), device_id_type=MESH,
+        )
+
+    for steps_x in halves_of_x:
+        for step_x in steps_x:
+            for step_y in range(row_y):
+                if step_y or step_x:
+                    turn_arrival(ROW_X * step_y + step_x).wait_recv()
+            pair_copy(step_x, core).start()
+    for step_x in range(ROW_X):
+        pair_copy(step_x, 1 - core).wait_recv()
     halves = jnp.concatenate([coarse_ref[c].reshape(groups * lam_dev, lanes) for c in range(2)], axis=1)
     even = jnp.dot(halves, to_even, preferred_element_type=F32)
     odd = jnp.dot(halves, to_odd, preferred_element_type=F32)
     for pair in range(groups // 2):
-        first = even[2 * pair * lam_dev : (2 * pair + 1) * lam_dev]
-        second = odd[(2 * pair + 1) * lam_dev : (2 * pair + 2) * lam_dev]
+        kept = [(number % ROW_X * row_y + number // ROW_X) * lam_dev for number in (2 * pair, 2 * pair + 1)]
+        first = even[kept[0] : kept[0] + lam_dev]
+        second = odd[kept[1] : kept[1] + lam_dev]
         base = pair * 3 * lanes
         ordered_ref[:, base : base + lanes] = first[:, :lanes]
         ordered_ref[:, base + lanes : base + 2 * lanes] = first[:, lanes:] + second[:, :lanes]
         ordered_ref[:, base + 2 * lanes : base + 3 * lanes] = second[:, lanes:]
 
-    pair_copy.wait_send()
-    lax.fori_loop(1, chips, sent(term_copy), 0)
+    for step_x in range(ROW_X):
+        pair_copy(step_x, core).wait_send()
+    for half in range(2):
+        lax.fori_loop(half * chips + 1, (half + 1) * chips, sent(term_copy), 0)
     lax.fori_loop(1, groups, sent(turn_copy), 0)
     lax.fori_loop(1, parts, sent(dual_copy), 0)
     lax.fori_loop(1, parts, arrived(dual_arrival), 0)
     for entry in range(refined_ref.shape[1]):
         blocks_ref[entry] = dual_ref[lax.shift_right_logical(refined_ref[0, entry], slots - 1)]
+
+
+def write_out(blocks_ref, ordered_ref, blocks_out, ordered_out, sem):
+    copies = []
+    for number, (source, target) in enumerate(((blocks_ref, blocks_out), (ordered_ref, ordered_out))):
+        half = source.shape[0] // 2
+        for at in range(2):
+            rows = pl.ds(at * half, half)
+            copies.append(pltpu.make_async_copy(source.at[rows], target.at[rows], sem.at[2 * number + at]))
+    for copy in copies:
+        copy.start()
+    for copy in copies:
+        copy.wait()
 
 
 def on_device(groups, parts, factor_inv, b_rows, b_coef, b_count, refined, modes, owner, lam_dev):
@@ -342,12 +378,12 @@
             pltpu.SemaphoreType.DMA((order // X_TILE,)),
             pltpu.SemaphoreType.DMA((parts,)),
             pltpu.SemaphoreType.DMA((parts,)),
-            pltpu.SemaphoreType.DMA((chips,)),
-            pltpu.SemaphoreType.DMA((chips,)),
+            pltpu.SemaphoreType.DMA((2 * chips,)),
+            pltpu.SemaphoreType.DMA((2 * chips,)),
             pltpu.SemaphoreType.DMA((groups,)),
             pltpu.SemaphoreType.DMA((groups,)),
-            pltpu.SemaphoreType.DMA,
-            pltpu.SemaphoreType.DMA,
+            pltpu.SemaphoreType.DMA((ROW_X,)),
+            pltpu.SemaphoreType.DMA((ROW_X,)),
             pltpu.SemaphoreType.REGULAR,
         ],
         compiler_params=pltpu.CompilerParams(
@@ -355,6 +391,18 @@
         ),
         name="assemble_and_send",
     )(*(pltpu.with_memory_space_constraint(array, pltpu.HBM) for array in inputs))
+    blocks, ordered = pl.pallas_call(
+        write_out,
+        out_shape=(
+            jax.ShapeDtypeStruct(blocks.shape, BF16),
+            jax.ShapeDtypeStruct(ordered.shape, F32),
+        ),
+        in_specs=[vmem, vmem],
+        out_specs=(anywhere, anywhere),
+        scratch_shapes=[pltpu.SemaphoreType.DMA((4,))],
+        compiler_params=pltpu.CompilerParams(vmem_limit_bytes=2 * 1024 * 1024),
+        name="write_out",
+    )(*(pltpu.with_memory_space_constraint(array, pltpu.VMEM) for array in (blocks, ordered)))
     return blocks, ordered.T
 
 

time: 32.9 us -> 31.8 us (0.967)
  local copies, waits for them, and re-layouts: 1.45 us -> 0 us
  Pallas kernels: 30.6 us -> 31 us
    unnamed x2 -> x0, local copies, waits for them, and re-layouts: 1.45 us -> none
    pallas_call x0 -> x1, Pallas kernels: none -> 0.87 us  [on_device(): pl.pallas_call(write_out, out_shape=(jax.ShapeDtypeStruct(blocks.shape, B...]
    pallas_call x1, Pallas kernels: 30.6 us -> 30.1 us  [on_device(): pl.pallas_call(functools.partial(assemble_and_send, groups, parts, lam_de...]
where the time goes in v3:
time: 31.8 us; the launch traced here: 31.6 us
  Pallas kernels  31 us (97%)
  between operations  0.64 us (2%)
    pallas_call x1, Pallas kernels, on_device(): pl.pallas_call(functools.partial(assemble_and_send, groups, parts, lam_de...  30.1 us
    pallas_call x1, Pallas kernels, on_device(): pl.pallas_call(write_out, out_shape=(jax.ShapeDtypeStruct(blocks.shape, B...  0.87 us

profile of v3, /device:TPU:1, one launch (start us, length us, event | category | flops | bytes accessed | tf_op | source)
XLA Modules:
  0.0 31.6 jit_solution(15335437334790626574)
XLA Ops:
  0.6 30.1 %assemble_and_send.1 = (bf16[8,32,512]{2,1,0:T(8,128)(2,1)S(1)}, f32[16,6144]{1,0:T(8,128)S(1)}) custom-call(s32[2]{0:T(128)} %count_hbm.1, s32[1,8]{1,0:T(1,128)} %refined_hbm.1, s32[2,512]{1,0:T(2,128)} %rows_hbm.1, f32[2,512]{1,0:T(2,128)} %coef_hbm.1, f32[6,2,1024]{2,1,0:T(2,128)} %bitcast.2, s32[2,512]{1,0:T(2,128)} %owner_hbm.1, ...), custom_call_target="tpu_custom_call" | custom-call | tf_op jit(solution)/shard_map/assemble_and_send/pallas_call | solution.py:351
  30.8 0.9 %write_out.1 = (bf16[8,32,512]{2,1,0:T(8,128)(2,1)}, f32[16,6144]{1,0:T(8,128)}) custom-call(bf16[8,32,512]{2,1,0:T(8,128)(2,1)S(1)} %get-tuple-element.6.blocks_ref, f32[16,6144]{1,0:T(8,128)S(1)} %get-tuple-element.7.ordered_ref), custom_call_target="tpu_custom_call" | custom-call | tf_op jit(solution)/shard_map/write_out/pallas_call | solution.py:394

commit v4 on v3

--- a/solution.py
+++ b/solution.py
@@ -78,16 +78,23 @@
 ):
     row = lax.axis_index("row")
     part = lax.axis_index("help")
-    core = part % 2
-    chip = part // 2
+    core = lax.rem(part, 2)
+    chip = lax.div(part, 2)
     chips = parts // 2
     slots, order, _ = factor_hbm.shape
     width = rows_ref.shape[1]
     modes = modes_ref.shape[0]
     lam = groups * lam_dev
     share = width // parts
-    y, x = row // ROW_X, row % ROW_X
+    y, x = lax.div(row, ROW_X), lax.rem(row, ROW_X)
     row_y = groups // ROW_X
+    chip_ahead = [lax.rem(chip + step, chips) for step in range(chips)]
+    chip_behind = [lax.rem(chip + chips - step, chips) for step in range(chips)]
+    core_at = [core, 1 - core]
+    y_ahead = [lax.rem(y + step, row_y) for step in range(row_y)]
+    y_behind = [lax.rem(y + row_y - step, row_y) for step in range(row_y)]
+    x_ahead = [lax.rem(x + step, ROW_X) for step in range(ROW_X)]
+    x_behind = [lax.rem(x + ROW_X - step, ROW_X) for step in range(ROW_X)]
     column_share = row_y * lam_dev
     half_width = lam // 2
 
@@ -109,7 +116,7 @@
     barrier = pltpu.get_barrier_semaphore()
 
     def greet_help(step, _):
-        pl.semaphore_signal(barrier, inc=1, device_id=(row, (part + step) % parts), device_id_type=MESH)
+        pl.semaphore_signal(barrier, inc=1, device_id=(row, lax.rem(part + step, parts)), device_id_type=MESH)
         return 0
 
     head = groups // 2
@@ -139,27 +146,9 @@
     term[...] = total
     terms[chip] = total
 
-    def start(copy):
-        def body(step, _):
-            copy(step).start()
-            return 0
-        return body
-
-    def arrived(copy):
-        def body(step, _):
-            copy(step).wait_recv()
-            return 0
-        return body
-
-    def sent(copy):
-        def body(step, _):
-            copy(step).wait_send()
-            return 0
-        return body
-
     def term_copy(step):
-        other = (chip + step % chips) % chips
-        at = pl.ds(pl.multiple_of(step // chips * half_width, half_width), half_width)
+        other = chip_ahead[step % chips]
+        at = pl.ds(step // chips * half_width, half_width)
         return pltpu.make_async_remote_copy(
             src_ref=term.at[:, at], dst_ref=terms.at[chip, :, at],
             send_sem=send_term.at[step], recv_sem=recv_term.at[step],
@@ -167,8 +156,8 @@
         )
 
     def term_arrival(step):
-        other = (chip + chips - step % chips) % chips
-        at = pl.ds(pl.multiple_of(step // chips * half_width, half_width), half_width)
+        other = chip_behind[step % chips]
+        at = pl.ds(step // chips * half_width, half_width)
         return pltpu.make_async_remote_copy(
             src_ref=term.at[:, at], dst_ref=terms.at[other, :, at],
             send_sem=send_term.at[step], recv_sem=recv_term.at[step],
@@ -176,7 +165,7 @@
         )
 
     def row_is_here(step, _):
-        pl.semaphore_signal(row_ready, inc=1, device_id=((row + step) % groups, part), device_id_type=MESH)
+        pl.semaphore_signal(row_ready, inc=1, device_id=(lax.rem(row + step, groups), part), device_id_type=MESH)
         return 0
 
     def meet_and_send_terms():
@@ -214,7 +203,7 @@
         ).astype(BF16)
 
     def dual_copy(step):
-        other = (chip + step // 2) % chips * 2 + (core + step % 2) % 2
+        other = chip_ahead[step // 2] * 2 + core_at[step % 2]
         return pltpu.make_async_remote_copy(
             src_ref=gram.at[pl.ds(other * share, share), :], dst_ref=dual_ref.at[part],
             send_sem=send_dual.at[step], recv_sem=recv_dual.at[step],
@@ -222,7 +211,7 @@
         )
 
     def dual_arrival(step):
-        other = (chip + chips - step // 2) % chips * 2 + (core + step % 2) % 2
+        other = chip_behind[step // 2] * 2 + core_at[step % 2]
         return pltpu.make_async_remote_copy(
             src_ref=gram.at[pl.ds(other * share, share), :], dst_ref=dual_ref.at[other],
             send_sem=send_dual.at[step], recv_sem=recv_dual.at[step],
@@ -240,7 +229,7 @@
     lanes = chips * slots * SLOT_ROWS
 
     def turn_copy(step):
-        other_y, other_x = (y + step // ROW_X) % row_y, (x + step % ROW_X) % ROW_X
+        other_y, other_x = y_ahead[step // ROW_X], x_ahead[step % ROW_X]
         start_row = (ROW_X + 2 - step % ROW_X) % ROW_X * column_share + other_y * lam_dev
         return pltpu.make_async_remote_copy(
             src_ref=turned.at[pl.ds(pl.multiple_of(start_row, lam_dev), lam_dev), :],
@@ -250,7 +239,7 @@
         )
 
     def turn_arrival(step):
-        other_y, other_x = (y + row_y - step // ROW_X) % row_y, (x + ROW_X - step % ROW_X) % ROW_X
+        other_y, other_x = y_behind[step // ROW_X], x_behind[step % ROW_X]
         return pltpu.make_async_remote_copy(
             src_ref=turned.at[pl.ds(0, lam_dev), :], dst_ref=coarse_ref.at[core, other_x * row_y + other_y],
             send_sem=send_turn.at[step], recv_sem=recv_turn.at[step],
@@ -263,7 +252,8 @@
 
     halves_of_x = ((2, 1), (0, 3))
     for half, steps_x in enumerate(halves_of_x):
-        lax.fori_loop(half * chips + 1, (half + 1) * chips, arrived(term_arrival), 0)
+        for step in range(1, chips):
+            term_arrival(half * chips + step).wait_recv()
         at = slice(half * half_width, (half + 1) * half_width)
         beside = terms[:, :, at].reshape(lanes, half_width)
         turned[at, :] = jnp.transpose(beside.astype(F32)).astype(BF16)
@@ -284,7 +274,7 @@
     there = chip * 2 + 1 - core
 
     def pair_copy(step_x, half):
-        at = pl.ds((x + ROW_X - step_x) % ROW_X * row_y, row_y)
+        at = pl.ds(x_behind[step_x] * row_y, row_y)
         return pltpu.make_async_remote_copy(
             src_ref=coarse_ref.at[half, at], dst_ref=coarse_ref.at[half, at],
             send_sem=send_pair.at[step_x], recv_sem=recv_pair.at[step_x],
@@ -297,6 +287,11 @@
                 if step_y or step_x:
                     turn_arrival(ROW_X * step_y + step_x).wait_recv()
             pair_copy(step_x, core).start()
+    for half in range(2):
+        for step in range(1, chips):
+            term_copy(half * chips + step).wait_send()
+    for step in range(1, groups):
+        turn_copy(step).wait_send()
     for step_x in range(ROW_X):
         pair_copy(step_x, 1 - core).wait_recv()
     halves = jnp.concatenate([coarse_ref[c].reshape(groups * lam_dev, lanes) for c in range(2)], axis=1)
@@ -313,11 +308,10 @@
 
     for step_x in range(ROW_X):
         pair_copy(step_x, core).wait_send()
-    for half in range(2):
-        lax.fori_loop(half * chips + 1, (half + 1) * chips, sent(term_copy), 0)
-    lax.fori_loop(1, groups, sent(turn_copy), 0)
-    lax.fori_loop(1, parts, sent(dual_copy), 0)
-    lax.fori_loop(1, parts, arrived(dual_arrival), 0)
+    for step in range(1, parts):
+        dual_copy(step).wait_send()
+    for step in range(1, parts):
+        dual_arrival(step).wait_recv()
     for entry in range(refined_ref.shape[1]):
         blocks_ref[entry] = dual_ref[lax.shift_right_logical(refined_ref[0, entry], slots - 1)]
 

time: 31.8 us -> 31.4 us (0.987)
  Pallas kernels: 31 us -> 30.6 us
    pallas_call x1, Pallas kernels: 30.1 us -> 29.7 us  [on_device(): pl.pallas_call(functools.partial(assemble_and_send, groups, parts, lam_de...]
where the time goes in v4:
time: 31.4 us; the launch traced here: 31.2 us
  Pallas kernels  30.6 us (97%)
  between operations  0.64 us (2%)
    pallas_call x1, Pallas kernels, on_device(): pl.pallas_call(functools.partial(assemble_and_send, groups, parts, lam_de...  29.7 us
    pallas_call x1, Pallas kernels, on_device(): pl.pallas_call(write_out, out_shape=(jax.ShapeDtypeStruct(blocks.shape, B...  0.87 us

profile of v4, /device:TPU:1, one launch (start us, length us, event | category | flops | bytes accessed | tf_op | source)
XLA Modules:
  0.0 31.2 jit_solution(3390872343953110873)
XLA Ops:
  0.6 29.7 %assemble_and_send.1 = (bf16[8,32,512]{2,1,0:T(8,128)(2,1)S(1)}, f32[16,6144]{1,0:T(8,128)S(1)}) custom-call(s32[2]{0:T(128)} %count_hbm.1, s32[1,8]{1,0:T(1,128)} %refined_hbm.1, s32[2,512]{1,0:T(2,128)} %rows_hbm.1, f32[2,512]{1,0:T(2,128)} %coef_hbm.1, f32[6,2,1024]{2,1,0:T(2,128)} %bitcast.2, s32[2,512]{1,0:T(2,128)} %owner_hbm.1, ...), custom_call_target="tpu_custom_call" | custom-call | tf_op jit(solution)/shard_map/assemble_and_send/pallas_call | solution.py:345
  30.4 0.9 %write_out.1 = (bf16[8,32,512]{2,1,0:T(8,128)(2,1)}, f32[16,6144]{1,0:T(8,128)}) custom-call(bf16[8,32,512]{2,1,0:T(8,128)(2,1)S(1)} %get-tuple-element.6.blocks_ref, f32[16,6144]{1,0:T(8,128)S(1)} %get-tuple-element.7.ordered_ref), custom_call_target="tpu_custom_call" | custom-call | tf_op jit(solution)/shard_map/write_out/pallas_call | solution.py:388

commit v5 on v4

--- a/solution.py
+++ b/solution.py
@@ -14,6 +14,7 @@
 LANES = 128
 X_TILE = 256
 GRAM_TILE = 256
+FIRST_CHIPS = 1
 VMEM_LIMIT = 28 * 1024 * 1024
 ROW_X = 4
 
@@ -146,15 +147,18 @@
     term[...] = total
     terms[chip] = total
 
-    def term_copy(step):
-        other = chip_ahead[step % chips]
-        at = pl.ds(step // chips * half_width, half_width)
+    def term_copy_to(other, half):
+        step = lax.rem(other + chips - chip, chips) + half * chips
+        at = pl.ds(half * half_width, half_width)
         return pltpu.make_async_remote_copy(
             src_ref=term.at[:, at], dst_ref=terms.at[chip, :, at],
             send_sem=send_term.at[step], recv_sem=recv_term.at[step],
             device_id=(row, other * 2 + core), device_id_type=MESH,
         )
 
+    def term_copy(step):
+        return term_copy_to(chip_ahead[step % chips], step // chips)
+
     def term_arrival(step):
         other = chip_behind[step % chips]
         at = pl.ds(step // chips * half_width, half_width)
@@ -176,8 +180,10 @@
             lax.fori_loop(1, groups, row_is_here, 0)
 
         for half in range(2):
-            for (step,) in far_first([(z,) for z in range(chips)], (chips,)):
-                term_copy(half * chips + step).start()
+            for other in range(chips):
+                @pl.when(other != chip)
+                def _(other=other, half=half):
+                    term_copy_to(other, half).start()
 
     late = chip >= chips // 2
 
@@ -202,14 +208,18 @@
             panel[:, at], panel[...], (((0,), (0,)), ((), ())), preferred_element_type=F32
         ).astype(BF16)
 
-    def dual_copy(step):
-        other = chip_ahead[step // 2] * 2 + core_at[step % 2]
+    def dual_copy_to(other_chip, other_core):
+        step = lax.rem(other_chip + chips - chip, chips) * 2 + other_core
+        other = other_chip * 2 + core_at[other_core]
         return pltpu.make_async_remote_copy(
             src_ref=gram.at[pl.ds(other * share, share), :], dst_ref=dual_ref.at[part],
             send_sem=send_dual.at[step], recv_sem=recv_dual.at[step],
             device_id=(row, other), device_id_type=MESH,
         )
 
+    def dual_copy(step):
+        return dual_copy_to(chip_ahead[step // 2], step % 2)
+
     def dual_arrival(step):
         other = chip_behind[step // 2] * 2 + core_at[step % 2]
         return pltpu.make_async_remote_copy(
@@ -222,8 +232,20 @@
     def _():
         meet_and_send_terms()
 
+    for other_chip in range(FIRST_CHIPS):
+        @pl.when(other_chip != chip)
+        def _(other_chip=other_chip):
+            for other_core in range(2):
+                dual_copy_to(other_chip, other_core).start()
+
     for z, other_core in far_first([(z, c) for z in range(chips) for c in range(2)], (chips, 2)):
-        dual_copy(2 * z + other_core).start()
+        if z == 0:
+            dual_copy(other_core).start()
+            continue
+
+        @pl.when(chip_ahead[z] >= FIRST_CHIPS)
+        def _(z=z, other_core=other_core):
+            dual_copy(2 * z + other_core).start()
     dual_ref[part] = gram[pl.ds(part * share, share), :]
 
     lanes = chips * slots * SLOT_ROWS

time: 31.4 us -> 30.9 us (0.984)
  Pallas kernels: 30.6 us -> 30.1 us
    pallas_call x1, Pallas kernels: 29.7 us -> 29.3 us  [on_device(): pl.pallas_call(functools.partial(assemble_and_send, groups, parts, lam_de...]
where the time goes in v5:
time: 30.9 us; the launch traced here: 30.8 us
  Pallas kernels  30.1 us (97%)
  between operations  0.64 us (2%)
    pallas_call x1, Pallas kernels, on_device(): pl.pallas_call(functools.partial(assemble_and_send, groups, parts, lam_de...  29.3 us
    pallas_call x1, Pallas kernels, on_device(): pl.pallas_call(write_out, out_shape=(jax.ShapeDtypeStruct(blocks.shape, B...  0.87 us

profile of v5, /device:TPU:1, one launch (start us, length us, event | category | flops | bytes accessed | tf_op | source)
XLA Modules:
  0.0 30.8 jit_solution(6739532579571588529)
XLA Ops:
  0.6 29.3 %assemble_and_send.1 = (bf16[8,32,512]{2,1,0:T(8,128)(2,1)S(1)}, f32[16,6144]{1,0:T(8,128)S(1)}) custom-call(s32[2]{0:T(128)} %count_hbm.1, s32[1,8]{1,0:T(1,128)} %refined_hbm.1, s32[2,512]{1,0:T(2,128)} %rows_hbm.1, f32[2,512]{1,0:T(2,128)} %coef_hbm.1, f32[6,2,1024]{2,1,0:T(2,128)} %bitcast.2, s32[2,512]{1,0:T(2,128)} %owner_hbm.1, ...), custom_call_target="tpu_custom_call" | custom-call | tf_op jit(solution)/shard_map/assemble_and_send/pallas_call | solution.py:367
  29.9 0.9 %write_out.1 = (bf16[8,32,512]{2,1,0:T(8,128)(2,1)}, f32[16,6144]{1,0:T(8,128)}) custom-call(bf16[8,32,512]{2,1,0:T(8,128)(2,1)S(1)} %get-tuple-element.6.blocks_ref, f32[16,6144]{1,0:T(8,128)S(1)} %get-tuple-element.7.ordered_ref), custom_call_target="tpu_custom_call" | custom-call | tf_op jit(solution)/shard_map/write_out/pallas_call | solution.py:410

commit v6 on v5

--- a/solution.py
+++ b/solution.py
@@ -179,10 +179,10 @@
         def _():
             lax.fori_loop(1, groups, row_is_here, 0)
 
-        for half in range(2):
-            for other in range(chips):
-                @pl.when(other != chip)
-                def _(other=other, half=half):
+        for other in range(chips):
+            @pl.when(other != chip)
+            def _(other=other):
+                for half in range(2):
                     term_copy_to(other, half).start()
 
     late = chip >= chips // 2

time: 30.9 us -> 30.8 us (level)
  no operation moved by 1% of the time
where the time goes in v6:
time: 30.8 us; the launch traced here: 30.7 us
  Pallas kernels  30 us (97%)
  between operations  0.64 us (2%)
    pallas_call x1, Pallas kernels, on_device(): pl.pallas_call(functools.partial(assemble_and_send, groups, parts, lam_de...  29.1 us
    pallas_call x1, Pallas kernels, on_device(): pl.pallas_call(write_out, out_shape=(jax.ShapeDtypeStruct(blocks.shape, B...  0.87 us

profile of v6, /device:TPU:1, one launch (start us, length us, event | category | flops | bytes accessed | tf_op | source)
XLA Modules:
  0.0 30.7 jit_solution(1416402838576026387)
XLA Ops:
  0.6 29.1 %assemble_and_send.1 = (bf16[8,32,512]{2,1,0:T(8,128)(2,1)S(1)}, f32[16,6144]{1,0:T(8,128)S(1)}) custom-call(s32[2]{0:T(128)} %count_hbm.1, s32[1,8]{1,0:T(1,128)} %refined_hbm.1, s32[2,512]{1,0:T(2,128)} %rows_hbm.1, f32[2,512]{1,0:T(2,128)} %coef_hbm.1, f32[6,2,1024]{2,1,0:T(2,128)} %bitcast.2, s32[2,512]{1,0:T(2,128)} %owner_hbm.1, ...), custom_call_target="tpu_custom_call" | custom-call | tf_op jit(solution)/shard_map/assemble_and_send/pallas_call | solution.py:367
  29.8 0.9 %write_out.1 = (bf16[8,32,512]{2,1,0:T(8,128)(2,1)}, f32[16,6144]{1,0:T(8,128)}) custom-call(bf16[8,32,512]{2,1,0:T(8,128)(2,1)S(1)} %get-tuple-element.6.blocks_ref, f32[16,6144]{1,0:T(8,128)S(1)} %get-tuple-element.7.ordered_ref), custom_call_target="tpu_custom_call" | custom-call | tf_op jit(solution)/shard_map/write_out/pallas_call | solution.py:410
